TPU v7x, 256 devices: a whole 4x4x8 slice. The times are simulated.
256 devices in a mesh: row: 16 (over x, y_lo, core), col: 16 (over z, y_hi).
Axes of the slice: x: 4, y: 4 (y_hi: 2, y_lo: 2; y = y_hi * 2 + y_lo), z: 8, core: 2. Of those that a mesh axis runs over, the one named last changes fastest.
Arguments:
- inputs: bfloat16 [2048, 12288], P('row', 'col'), may hold values from -6 to 6
- w_up: bfloat16 [12288, 12288], P('col', 'row'), may hold values from -0.0546875 to 0.0546875
- w_down: bfloat16 [12288, 12288], P('row', 'col'), may hold values from -0.0546875 to 0.0546875
- upstream: bfloat16 [2048, 12288], P('row', 'col'), may hold values from -6 to 6
Outputs:
- grad_input: bfloat16 [2048, 12288], P('row', 'col')
- grad_up: bfloat16 [12288, 12288], P('col', 'row')
- grad_down: bfloat16 [12288, 12288], P('row', 'col')
All inputs are finite; a program needn't handle non-finite values.
Results may differ from a plain program's by a relative error of at most 0.034.
Values may be sent and summed in bfloat16 or wider, within the bound.
A program may use at most 64 MiB of HBM per device.

v0:
```python
import math

import jax
import jax.numpy as jnp
from jax import lax
from jax.sharding import PartitionSpec as P


def gelu_parts(preact):
    coeff = math.sqrt(2.0 / math.pi)
    cubic = 0.044715
    inner = coeff * (preact + cubic * preact * preact * preact)
    tangent = jnp.tanh(inner)
    value = 0.5 * preact * (1.0 + tangent)
    slope = 0.5 * (1.0 + tangent) + 0.5 * preact * (1.0 - tangent * tangent) * coeff * (
        1.0 + 3.0 * cubic * preact * preact
    )
    return (value, slope)


def contract_first(left, right):
    return lax.dot_general(
        left, right, (((0,), (0,)), ((), ())), preferred_element_type=jnp.float32
    )


def contract_last(left, right):
    return lax.dot_general(
        left, right, (((1,), (1,)), ((), ())), preferred_element_type=jnp.float32
    )


def on_device(inputs, w_up, w_down, upstream):
    gathered_in, gathered_grad = (
        lax.all_gather(inputs, "row", axis=0, tiled=True),
        lax.all_gather(upstream, "row", axis=0, tiled=True),
    )
    tokens = gathered_in.shape[0]
    piece = gathered_in
    preact = lax.psum_scatter(
        jnp.dot(piece, w_up, preferred_element_type=jnp.float32).astype(jnp.bfloat16),
        "col",
        scatter_dimension=0,
        tiled=True,
    ).astype(jnp.float32)
    activation, slope = gelu_parts(preact)
    act_low = activation.astype(jnp.bfloat16)
    down_total = contract_first(lax.all_gather(act_low, "col", axis=0, tiled=True), gathered_grad)
    piece = gathered_grad
    grad_act = lax.psum_scatter(
        contract_last(piece, w_down).astype(jnp.bfloat16), "col", scatter_dimension=0, tiled=True
    ).astype(jnp.float32)
    grad_pre = (grad_act * slope).astype(jnp.bfloat16)
    grad_pre_all = lax.all_gather(grad_pre, "col", axis=0, tiled=True)
    up_total = contract_first(gathered_in, grad_pre_all)
    piece = grad_pre_all
    grad_input = lax.psum_scatter(
        contract_last(piece, w_up).astype(jnp.bfloat16), "row", scatter_dimension=0, tiled=True
    )
    factor = 1.0 / math.sqrt(tokens)
    grad_up = (up_total * factor).astype(jnp.bfloat16)
    grad_down = (down_total * factor).astype(jnp.bfloat16)
    return (grad_input, grad_up, grad_down)


def solution(mesh):
    in_specs = (P("row", "col"), P("col", "row"), P("row", "col"), P("row", "col"))
    out_specs = (P("row", "col"), P("col", "row"), P("row", "col"))
    return jax.shard_map(
        on_device, mesh=mesh, in_specs=in_specs, out_specs=out_specs, check_vma=False
    )
```

profile of v0, /device:TPU:6, one launch (start us, length us, event | category | flops | bytes accessed | tf_op | source)
XLA Modules:
  0.0 773.7 jit_solution(13669342803071558074)
XLA Ops:
  7.2 0.0 copy-start
  7.2 0.0 all-gather.5.cloned.1.call-start
  7.2 0.7 all-gather.5.cloned.1.call-update
  7.9 0.0 all-gather.7.cloned.1.call-start
  8.0 0.7 all-gather.7.cloned.1.call-update
  8.7 0.0 reduce-scatter.4.cloned.1.call-start
  8.7 41.6 %all-gather.5.cloned.1.call-done = bf16[2048,768]{1,0:T(8,128)(2,1)} async-done(((bf16[128,768]{1,0:T(8,128)(2,1)}), bf16[2048,768]{1,0:T(8,128)(2,1)}) %all-gather.5.cloned.1.call-update) | async-done | bytes 3145744 | tf_op jit(solution)/shard_map/all_gather | solution.py:36
  50.3 6.6 convolution_convert_fusion.2
  56.9 0.0 reduce-scatter.4.cloned.1.call-update
  56.9 0.0 reduce-scatter.6.cloned.1.call-start
  56.9 33.8 %all-gather.7.cloned.1.call-done = bf16[2048,768]{1,0:T(8,128)(2,1)} async-done(((bf16[128,768]{1,0:T(8,128)(2,1)}), bf16[2048,768]{1,0:T(8,128)(2,1)}) %all-gather.7.cloned.1.call-update) | async-done | bytes 3145744 | tf_op jit(solution)/shard_map/all_gather | solution.py:35
  90.7 0.0 copy-done
  90.7 6.2 convolution_convert_fusion.1
  96.9 0.0 reduce-scatter.6.cloned.1.call-update
  96.9 0.0 all-gather.9.cloned.1.call-start
  96.9 208.8 %reduce-scatter.4.cloned.1.call-done = bf16[128,768]{1,0:T(8,128)(2,1)} async-done(((bf16[2048,768]{1,0:T(8,128)(2,1)}), bf16[128,768]{1,0:T(8,128)(2,1)}) %reduce-scatter.4.cloned.1.call-update) | async-done | bytes 196624 | tf_op jit(solution)/shard_map/reduce_scatter | solution.py:50
  305.8 212.4 %reduce-scatter.6.cloned.1.call-done = bf16[128,768]{1,0:T(8,128)(2,1)} async-done(((bf16[2048,768]{1,0:T(8,128)(2,1)}), bf16[128,768]{1,0:T(8,128)(2,1)}) %reduce-scatter.6.cloned.1.call-update) | async-done | bytes 196624 | tf_op jit(solution)/shard_map/reduce_scatter | solution.py:40
  518.1 2.1 fusion.8
  520.2 0.0 all-gather.9.cloned.1.call-update
  520.2 0.0 all-gather.11.cloned.1.call-start
  520.3 0.5 all-gather.11.cloned.1.call-update
  520.8 0.2 reduce-scatter.8.cloned.1.call-start
  521.0 91.5 %all-gather.9.cloned.1.call-done = bf16[2048,768]{1,0:T(8,128)(2,1)} async-done(((bf16[128,768]{1,0:T(8,128)(2,1)}), bf16[2048,768]{1,0:T(8,128)(2,1)}) %all-gather.9.cloned.1.call-update) | async-done | bytes 3145744 | tf_op jit(solution)/shard_map/all_gather | solution.py:54
  612.5 6.2 convolution_convert_fusion
  618.7 0.0 reduce-scatter.8.cloned.1.call-update
  618.7 5.5 fusion
  624.2 1.5 copy.7
  625.7 79.7 %all-gather.11.cloned.1.call-done = bf16[2048,768]{1,0:T(8,128)(2,1)} async-done(((bf16[128,768]{1,0:T(8,128)(2,1)}), bf16[2048,768]{1,0:T(8,128)(2,1)}) %all-gather.11.cloned.1.call-update) | async-done | bytes 3145744 | tf_op jit(solution)/shard_map/all_gather | solution.py:48
  705.4 6.5 multiply_convert_fusion
  711.9 54.9 %reduce-scatter.8.cloned.1.call-done = bf16[128,768]{1,0:T(8,128)(2,1)} async-done(((bf16[2048,768]{1,0:T(8,128)(2,1)}), bf16[128,768]{1,0:T(8,128)(2,1)}) %reduce-scatter.8.cloned.1.call-update) | async-done | bytes 196624 | tf_op jit(solution)/shard_map/reduce_scatter | solution.py:57
Async XLA Ops:
  7.2 83.5 %copy-start = (bf16[768,768]{1,0:T(8,128)(2,1)S(1)}, bf16[768,768]{1,0:T(8,128)(2,1)}, u32[]{:S(2)}) copy-start(bf16[768,768]{1,0:T(8,128)(2,1)} %param.5) | copy-start | bytes 3538948
  7.2 43.1 %all-gather.5.cloned.1.call-start = ((), (), s32[]{:S(2)}) async-start(), calls=%async_computation.3 | async-start | bytes 3342336 | tf_op jit(solution)/shard_map/all_gather | solution.py:36
  7.9 82.8 %all-gather.7.cloned.1.call-start = ((), (), s32[]{:S(2)}) async-start(), calls=%async_computation.5 | async-start | bytes 3342336 | tf_op jit(solution)/shard_map/all_gather | solution.py:35
  8.7 297.1 %reduce-scatter.4.cloned.1.call-start = ((), (), s32[]{:S(2)}) async-start(), calls=%async_computation.4 | async-start | bytes 3342336 | tf_op jit(solution)/shard_map/reduce_scatter | solution.py:50
  56.9 461.3 %reduce-scatter.6.cloned.1.call-start = ((), (), s32[]{:S(2)}) async-start(), calls=%async_computation.6 | async-start | bytes 3342336 | tf_op jit(solution)/shard_map/reduce_scatter | solution.py:40
  96.9 515.6 %all-gather.9.cloned.1.call-start = ((), (), s32[]{:S(2)}) async-start(), calls=%async_computation.7 | async-start | bytes 3342336 | tf_op jit(solution)/shard_map/all_gather | solution.py:54
  520.2 185.2 %all-gather.11.cloned.1.call-start = ((), (), s32[]{:S(2)}) async-start(), calls=%async_computation.9 | async-start | bytes 3342336 | tf_op jit(solution)/shard_map/all_gather | solution.py:48
  520.8 246.0 %reduce-scatter.8.cloned.1.call-start = ((), (), s32[]{:S(2)}) async-start(), calls=%async_computation.8 | async-start | bytes 3342336 | tf_op jit(solution)/shard_map/reduce_scatter | solution.py:57
Sparse Core Ops, SparseCore 0:
  9.9 40.3 all-gather.4
  52.1 38.5 all-gather.6
  94.7 211.0 reduce-scatter.3
  310.1 207.9 reduce-scatter.5
  521.2 91.2 all-gather.8
  615.5 89.8 all-gather.10
  708.5 58.2 reduce-scatter.7
where the time goes:
time: 780 us; the launch traced here: 774 us
  waiting for transfers between devices  725 us (93%)
  matrix products  31 us (4%)
  between operations  14.1 us (2%)
    reduce_scatter x1, waiting for transfers between devices, on_device(): lax.psum_scatter(jnp.dot(piece, w_up, preferred_element_type=jnp.float32)...  212 us
    reduce_scatter x1, waiting for transfers between devices, on_device(): lax.psum_scatter(contract_last(piece, w_down).astype(jnp.bfloat16), 'col'...  209 us
    all_gather x1, waiting for transfers between devices, on_device(): grad_pre_all = lax.all_gather(grad_pre, 'col', axis=0, tiled=True)  91.5 us
    all_gather x1, waiting for transfers between devices, on_device(): lax.all_gather(act_low, 'col', axis=0, tiled=True)  79.7 us
    reduce_scatter x1, waiting for transfers between devices, on_device(): lax.psum_scatter(contract_last(piece, w_up).astype(jnp.bfloat16), 'row',...  54.9 us
    all_gather x1, waiting for transfers between devices, on_device(): lax.all_gather(upstream, 'row', axis=0, tiled=True)  41.6 us
    all_gather x1, waiting for transfers between devices, on_device(): lax.all_gather(inputs, 'row', axis=0, tiled=True)  33.8 us
  transfers between devices with their start and end apart: 7, of which 7 were waited for; matrix products, arithmetic and copies ran while one was open for 4% of the time, Pallas kernels for 0%

commit v1 on v0

v1 whole, which is shorter than its diff:
```python
import functools
import math

import jax
import jax.numpy as jnp
from jax import lax
from jax.experimental import pallas as pl
from jax.experimental.pallas import tpu as pltpu
from jax.sharding import PartitionSpec as P

MESH = pl.DeviceIdType.MESH
BF = jnp.bfloat16
F32 = jnp.float32
RING = 8
HALF = 64
ORDER = (0, 2, 1, 3)


def mod8(value):
    return lax.rem(value + 64, 8)


def gelu_parts(preact):
    coeff = math.sqrt(2.0 / math.pi)
    cubic = 0.044715
    inner = coeff * (preact + cubic * preact * preact * preact)
    tangent = jnp.tanh(inner)
    value = 0.5 * preact * (1.0 + tangent)
    slope = 0.5 * (1.0 + tangent) + 0.5 * preact * (1.0 - tangent * tangent) * coeff * (
        1.0 + 3.0 * cubic * preact * preact
    )
    return (value, slope)


def dot(left, right, left_dim, right_dim):
    return lax.dot_general(
        left, right, (((left_dim,), (right_dim,)), ((), ())), preferred_element_type=F32
    )


def kernel(
    x_ref, wu_ref, wd_ref, g_ref,
    gi_ref, gu_ref, gd_ref,
    gath, part, rs_out, rs_in, fin, y_out, y_in, slope_ref, ag, acc_up, acc_down,
    gi_keep, gi_sib_out, gi_sib_in, gi_out, gi_in,
    gath_ss, gath_rs, sib_ss, sib_rs, rs_ss, rs_rs, y_ss, y_rs, agy_ss, agy_rs, ag_ss, ag_rs,
    gs_ss, gs_rs, gi_ss, gi_rs,
):
    r, c = lax.axis_index("row"), lax.axis_index("col")
    o, p = lax.div(r, 2), lax.rem(r, 2)
    z, yh = lax.div(c, 2), lax.rem(c, 2)
    sign = 1 - 2 * p
    up = (r, lax.rem(c + 2, 16))
    down = (r, lax.rem(c + 14, 16))
    partner = (r, c + 1 - 2 * yh)
    sibling = (r + 1 - 2 * p, c)

    def peer(index):
        return (2 * index + p, c)

    def remote(src, dst, send, recv, device):
        return pltpu.make_async_remote_copy(
            src_ref=src, dst_ref=dst, send_sem=send, recv_sem=recv,
            device_id=device, device_id_type=MESH,
        )

    barrier = pltpu.get_barrier_semaphore()
    for device in (up, down, partner, sibling):
        pl.semaphore_signal(barrier, inc=1, device_id=device, device_id_type=MESH)
    for k in range(1, 8):
        pl.semaphore_signal(
            barrier, inc=1, device_id=peer(mod8(o + k)), device_id_type=MESH
        )
    pl.semaphore_wait(barrier, 11)

    def block_of(s, direction):
        if direction == 0:
            return 2 * mod8(o + z - 1 - s)
        return 2 * mod8(o + z + 1 + s) + 1

    def zed(s, direction):
        return mod8(z - 1 - s) if direction == 0 else mod8(z + 1 + s)

    def gather_copy(a, s):
        to = mod8(o - z + sign * (1 + s))
        own = x_ref if a == 0 else g_ref
        return to, remote(
            own, gath.at[a, r], gath_ss.at[a, s], gath_rs.at[a, o], peer(to)
        )

    for a in range(2):
        for s in range(8):
            to, copy = gather_copy(a, s)

            @pl.when(to != o)
            def _(copy=copy):
                copy.start()

    gath[0, r] = x_ref[...]
    gath[1, r] = g_ref[...]

    def direct_index(s):
        return mod8(o + z - sign * (1 + s))

    def forward(a, s):
        source = direct_index(s)
        block = 2 * source + p

        @pl.when(source != o)
        def _():
            remote(
                gath.at[a, block], gath.at[a, block], gath_ss.at[a, 0],
                gath_rs.at[a, source], sibling,
            ).wait_recv()

        remote(
            gath.at[a, block], gath.at[a, block], sib_ss.at[a, s], sib_rs.at[a, s], sibling
        ).start()

    def sibling_wait(a, s):
        block = 2 * mod8(o + z + sign * (1 + s)) + 1 - p
        remote(
            gath.at[a, block], gath.at[a, block], sib_ss.at[a, s], sib_rs.at[a, s], sibling
        ).wait_recv()

    def pair(a, s):
        return jnp.concatenate(
            [gath[a, block_of(s, 0)], gath[a, block_of(s, 1)]], axis=0
        )

    def ring_copy(a, s, q):
        return remote(
            rs_out.at[a, s, q], rs_in.at[a, s, q], rs_ss.at[a, s, q], rs_rs.at[a, s, q],
            up if q < 2 else down,
        )

    def partial(a, s):
        if a == 0:
            return dot(pair(0, s), wu_ref[...], 1, 0)
        return dot(pair(1, s), wd_ref[...], 1, 1)

    def reduce_step(a, s):
        sibling_wait(a, s)
        part[...] = partial(a, s)

        @pl.when(s < 7)
        def _():
            forward(a, s + 1)

        for q in ORDER:
            rows = pl.ds(q * HALF, HALF)

            @pl.when(s == 0)
            def _():
                rs_out[a, 0, q] = part[rows, :].astype(BF)

            @pl.when(s > 0)
            def _():
                ring_copy(a, s - 1, q).wait_recv()
                total = part[rows, :] + rs_in[a, s - 1, q].astype(F32)

                @pl.when(s < 7)
                def _():
                    rs_out[a, s, q] = total.astype(BF)

                @pl.when(s == 7)
                def _():
                    fin[a, rows, :] = total
                    y_out[a, rows, :] = total.astype(BF)

            @pl.when(s < 7)
            def _():
                ring_copy(a, s, q).start()

    def y_copy(a):
        return remote(
            y_out.at[a, pl.ds((1 - yh) * 128, 128)], y_in.at[a], y_ss.at[a], y_rs.at[a], partner
        )

    def reduced(a):
        y_copy(a).wait_recv()
        return fin[a, pl.ds(yh * 128, 128), :] + y_in[a].astype(F32)

    def agy_copy(a):
        return remote(ag.at[a, z, yh], ag.at[a, z, yh], agy_ss.at[a], agy_rs.at[a], partner)

    def agy_wait(a):
        remote(
            ag.at[a, z, 1 - yh], ag.at[a, z, 1 - yh], agy_ss.at[a], agy_rs.at[a], partner
        ).wait_recv()

    def ag_first(a, direction):
        for half in range(2):
            piece = ag.at[a, z, direction, pl.ds(half * HALF, HALF)]
            q = 2 * direction + half
            remote(
                piece, piece, ag_ss.at[a, 0, q], ag_rs.at[a, 0, q],
                (r, lax.rem(c + 2 + 12 * direction, 16)),
            ).start()

    def ag_piece(a, s, q):
        direction, half = q // 2, q % 2
        return ag.at[a, zed(s, direction), direction, pl.ds(half * HALF, HALF)]

    def ag_step(a, s):
        for q in ORDER:
            piece = ag_piece(a, s, q)
            device = up if q < 2 else down
            remote(piece, piece, ag_ss.at[a, s, q], ag_rs.at[a, s, q], device).wait_recv()

            @pl.when(s < 6)
            def _():
                remote(
                    piece, piece, ag_ss.at[a, s + 1, q], ag_rs.at[a, s + 1, q], device
                ).start()

    def gathered(a, s):
        return jnp.concatenate([ag[a, zed(s, 0), 0], ag[a, zed(s, 1), 1]], axis=0)

    def accumulate(acc, left, right, first):
        for m in range(3):
            rows = pl.ds(m * 256, 256)
            term = dot(left[:, m * 256 : (m + 1) * 256], right, 0, 0)
            if first:
                acc[rows, :] = term
            else:
                acc[rows, :] += term

    def gi_dest(s):
        return mod8(o + z - sign * (1 + s))

    def gi_sib_copy(s):
        return remote(
            gi_sib_out.at[s], gi_sib_in.at[s], gs_ss.at[s], gs_rs.at[s], sibling
        )

    def gi_copy(s):
        return remote(
            gi_out.at[s], gi_in.at[o], gi_ss.at[s], gi_rs.at[o], peer(gi_dest(s))
        )

    def gi_start(s, rows_in):
        part[...] = dot(rows_in, wu_ref[...], 1, 1)
        gi_sib_out[s] = part[pl.ds((1 - p) * 128, 128), :].astype(BF)
        gi_sib_copy(s).start()
        gi_keep[s] = part[pl.ds(p * 128, 128), :]

    def gi_finish(s):
        gi_sib_copy(s).wait_recv()
        total = (gi_keep[s] + gi_sib_in[s].astype(F32)).astype(BF)
        dest = gi_dest(s)

        @pl.when(dest == o)
        def _():
            gi_in[o] = total

        @pl.when(dest != o)
        def _():
            gi_out[s] = total
            gi_copy(s).start()

    forward(0, 0)

    @pl.loop(0, 8)
    def _(s):
        reduce_step(0, s)

    y_copy(0).start()
    forward(1, 0)

    @pl.loop(0, 8)
    def _(s):
        reduce_step(1, s)

        @pl.when(s == 1)
        def _():
            value, slope = gelu_parts(reduced(0))
            slope_ref[...] = slope
            ag[0, z, yh] = value.astype(BF)
            agy_copy(0).start()

    y_copy(1).start()
    ag_first(0, yh)
    agy_wait(0)
    ag_first(0, 1 - yh)
    accumulate(acc_down, gathered(0, 7), pair(1, 7), True)

    @pl.loop(0, 7)
    def _(s):
        ag_step(0, s)

        @pl.when(s == 1)
        def _():
            ag[1, z, yh] = (reduced(1) * slope_ref[...]).astype(BF)
            agy_copy(1).start()

        accumulate(acc_down, gathered(0, s), pair(1, s), False)

    ag_first(1, yh)
    agy_wait(1)
    ag_first(1, 1 - yh)
    own_pre = gathered(1, 7)
    gi_start(7, own_pre)
    accumulate(acc_up, pair(0, 7), own_pre, True)
    gi_finish(7)
    factor = 1.0 / math.sqrt(2048)
    gd_ref[...] = (acc_down[...] * factor).astype(BF)

    @pl.loop(0, 7)
    def _(s):
        ag_step(1, s)
        pre = gathered(1, s)
        gi_start(s, pre)
        accumulate(acc_up, pair(0, s), pre, False)
        gi_finish(s)

    gu_ref[...] = (acc_up[...] * factor).astype(BF)

    total = gi_in[o].astype(F32)
    for k in range(1, 8):
        source = mod8(o + k)
        remote(
            gi_out.at[0], gi_in.at[source], gi_ss.at[0], gi_rs.at[source], sibling
        ).wait_recv()
        total += gi_in[source].astype(F32)
    gi_ref[...] = total.astype(BF)

    for a in range(2):
        y_copy(a).wait_send()
        agy_copy(a).wait_send()

        @pl.loop(0, 8)
        def _(s):
            to, copy = gather_copy(a, s)

            @pl.when(to != o)
            def _():
                copy.wait_send()

            remote(
                gath.at[a, 0], gath.at[a, 0], sib_ss.at[a, s], sib_rs.at[a, s], sibling
            ).wait_send()

        @pl.loop(0, 7)
        def _(s):
            for q in range(4):
                ring_copy(a, s, q).wait_send()
                piece = ag.at[a, 0, 0, pl.ds(0, HALF)]
                remote(
                    piece, piece, ag_ss.at[a, s, q], ag_rs.at[a, s, q], up
                ).wait_send()

    @pl.loop(0, 8)
    def _(s):
        gi_sib_copy(s).wait_send()

        @pl.when(gi_dest(s) != o)
        def _():
            gi_copy(s).wait_send()


def on_device(inputs, w_up, w_down, upstream):
    tokens, width = inputs.shape
    hidden = w_up.shape[1]
    dma = pltpu.SemaphoreType.DMA
    vmem = pl.BlockSpec(memory_space=pltpu.VMEM)
    return pl.pallas_call(
        kernel,
        out_shape=(
            jax.ShapeDtypeStruct((tokens, width), BF),
            jax.ShapeDtypeStruct((width, hidden), BF),
            jax.ShapeDtypeStruct((hidden, width), BF),
        ),
        in_specs=[vmem] * 4,
        out_specs=(vmem, vmem, vmem),
        scratch_shapes=[
            pltpu.VMEM((2, 16, 128, 768), BF),
            pltpu.VMEM((256, 768), F32),
            pltpu.VMEM((2, 7, 4, HALF, 768), BF),
            pltpu.VMEM((2, 7, 4, HALF, 768), BF),
            pltpu.VMEM((2, 256, 768), F32),
            pltpu.VMEM((2, 256, 768), BF),
            pltpu.VMEM((2, 128, 768), BF),
            pltpu.VMEM((128, 768), F32),
            pltpu.VMEM((2, 8, 2, 128, 768), BF),
            pltpu.VMEM((768, 768), F32),
            pltpu.VMEM((768, 768), F32),
            pltpu.VMEM((8, 128, 768), F32),
            pltpu.VMEM((8, 128, 768), BF),
            pltpu.VMEM((8, 128, 768), BF),
            pltpu.VMEM((8, 128, 768), BF),
            pltpu.VMEM((8, 128, 768), BF),
            dma((2, 8)), dma((2, 8)), dma((2, 8)), dma((2, 8)),
            dma((2, 7, 4)), dma((2, 7, 4)),
            dma((2,)), dma((2,)), dma((2,)), dma((2,)),
            dma((2, 7, 4)), dma((2, 7, 4)),
            dma((8,)), dma((8,)), dma((8,)), dma((8,)),
        ],
        compiler_params=pltpu.CompilerParams(
            collective_id=0, has_side_effects=True, vmem_limit_bytes=58 << 20
        ),
        cost_estimate=pl.CostEstimate(
            flops=5 * 2 * 2048 * 768 * 768, bytes_accessed=6 << 20, transcendentals=128 * 768
        ),
        name="block_backward",
    )(inputs, w_up, w_down, upstream)


def solution(mesh):
    in_specs = (P("row", "col"), P("col", "row"), P("row", "col"), P("row", "col"))
    out_specs = (P("row", "col"), P("col", "row"), P("row", "col"))
    return jax.shard_map(
        on_device, mesh=mesh, in_specs=in_specs, out_specs=out_specs, check_vma=False
    )
```

time: 780 us -> 187 us (0.24)
  waiting for transfers between devices: 725 us -> 0 us
  Pallas kernels: 0 us -> 178 us
  matrix products: 31 us -> 0 us
  between operations: 14.1 us -> 0.64 us
    reduce_scatter x3 -> x0, waiting for transfers between devices: 476 us -> none  [the longest x1 212 us: on_device(): lax.psum_scatter(jnp.dot(piece, w_up, preferred_element_type=jnp.float32)...]
    all_gather x4 -> x0, waiting for transfers between devices: 247 us -> none  [the longest x1 91.5 us: on_device(): grad_pre_all = lax.all_gather(grad_pre, 'col', axis=0, tiled=True)]
    pallas_call x0 -> x1, Pallas kernels: none -> 178 us  [on_device(): pl.pallas_call(kernel, out_shape=(jax.ShapeDtypeStruct((tokens, width), B...]
    dot_general x5 -> x0, matrix products: 31 us -> none  [the longest x2 12.8 us: contract_last(): lax.dot_general(left, right, (((1,), (1,)), ((), ())), preferred_element_...]
  transfers between devices with their start and end apart: 7 -> 0, of which waited for: 7 -> 0; matrix products, arithmetic and copies ran while one was open for 4% -> 0% of each run, Pallas kernels for 0% -> 0%
where the time goes in v1:
time: 187 us; the launch traced here: 184 us
  Pallas kernels  178 us (95%)
  local copies, waits for them, and re-layouts  5.09 us (3%)
    pallas_call x1, Pallas kernels, on_device(): pl.pallas_call(kernel, out_shape=(jax.ShapeDtypeStruct((tokens, width), B...  178 us
    unnamed x5, local copies, waits for them, and re-layouts  5.09 us

profile of v1, /device:TPU:6, one launch (start us, length us, event | category | flops | bytes accessed | tf_op | source)
XLA Modules:
  0.0 184.0 jit_solution(18325495089424717768)
XLA Ops:
  0.6 178.2 %block_backward.1 = (bf16[128,768]{1,0:T(8,128)(2,1)}, bf16[768,768]{1,0:T(8,128)(2,1)}, bf16[768,768]{1,0:T(8,128)(2,1)}) custom-call(bf16[128,768]{1,0:T(8,128)(2,1)} %x_ref.1, bf16[768,768]{1,0:T(8,128)(2,1)} %wu_ref.1, bf16[768,768]{1,0:T(8,128)(2,1)} %wd_ref.1, bf16[128,768]{1,0:T(8,128)(2,1)} %g_ref.1), custom_call_target="tpu_custom_call" | custom-call | flops 12079595520 | bytes 6291456 | tf_op jit(solution)/shard_map/block_backward/pallas_call | solution.py:367
  178.9 1.6 copy.10
  180.5 0.0 copy-start
  180.5 2.5 %copy.11 = bf16[768,768]{1,0:T(8,128)(2,1)} copy(bf16[768,768]{1,0:T(8,128)(2,1)} %get-tuple-element.7) | data formatting | bytes 2359296
  183.0 0.0 copy-done
  183.0 1.0 copy.12
Async XLA Ops:
  180.5 2.5 %copy-start = (bf16[768,768]{1,0:T(8,128)(2,1)S(1)}, bf16[768,768]{1,0:T(8,128)(2,1)}, u32[]{:S(2)}) copy-start(bf16[768,768]{1,0:T(8,128)(2,1)} %get-tuple-element.8) | copy-start | bytes 3538948

commit v2 on v0

v2 whole, which is shorter than its diff:
```python
import functools
import math

import jax
import jax.numpy as jnp
from jax import lax
from jax.experimental import pallas as pl
from jax.experimental.pallas import tpu as pltpu
from jax.sharding import PartitionSpec as P

MESH = pl.DeviceIdType.MESH
BF = jnp.bfloat16
F32 = jnp.float32
RING = 8
HALF = 64
REL = (4, 3, -3, 2, -2, 1, -1, 0)
PARTS = tuple((j, h) for j in range(2) for h in range(2))


def mod8(value):
    return lax.rem(value + 64, 8)


def gelu_parts(preact):
    coeff = math.sqrt(2.0 / math.pi)
    cubic = 0.044715
    inner = coeff * (preact + cubic * preact * preact * preact)
    tangent = jnp.tanh(inner)
    value = 0.5 * preact * (1.0 + tangent)
    slope = 0.5 * (1.0 + tangent) + 0.5 * preact * (1.0 - tangent * tangent) * coeff * (
        1.0 + 3.0 * cubic * preact * preact
    )
    return (value, slope)


def dot(left, right, left_dim, right_dim):
    return lax.dot_general(
        left, right, (((left_dim,), (right_dim,)), ((), ())), preferred_element_type=F32
    )


def kernel(
    x_ref, wu_ref, wd_ref, g_ref,
    gi_ref, gu_ref, gd_ref,
    gath, part, wu, wd, rs_out, rs_in, fin, y_out, y_in, slope_ref, ag, acc_up, acc_down,
    gi_sib_out, gi_sib_in, gi_out, gi_in,
    w_sem, gath_ss, gath_rs, sib_ss, sib_rs, rs_ss, rs_rs, y_ss, y_rs,
    agy_ss, agy_rs, ag_ss, ag_rs, gs_ss, gs_rs, gi_ss, gi_rs,
):
    r, c = lax.axis_index("row"), lax.axis_index("col")
    o, p = lax.div(r, 2), lax.rem(r, 2)
    z, yh = lax.div(c, 2), lax.rem(c, 2)
    along = ((r, lax.rem(c + 2, 16)), (r, lax.rem(c + 14, 16)))
    partner = (r, c + 1 - 2 * yh)
    sibling = (r + 1 - 2 * p, c)

    def peer(index):
        return (2 * index + p, c)

    def remote(src, dst, send, recv, device):
        return pltpu.make_async_remote_copy(
            src_ref=src, dst_ref=dst, send_sem=send, recv_sem=recv,
            device_id=device, device_id_type=MESH,
        )

    barrier = pltpu.get_barrier_semaphore()
    for device in along + (partner, sibling):
        pl.semaphore_signal(barrier, inc=1, device_id=device, device_id_type=MESH)
    for k in range(1, 8):
        pl.semaphore_signal(
            barrier, inc=1, device_id=peer(mod8(o + k)), device_id_type=MESH
        )
    w_copies = [
        pltpu.make_async_copy(wu_ref, wu, w_sem.at[0]),
        pltpu.make_async_copy(wd_ref, wd, w_sem.at[1]),
    ]
    for copy in w_copies:
        copy.start()
    gath[0, r] = x_ref[...]
    gath[1, r] = g_ref[...]
    pl.semaphore_wait(barrier, 11)

    def gather_copy(a, i):
        to = mod8(o - z - REL[i])
        return to, remote(
            gath.at[a, r], gath.at[a, r], gath_ss.at[a, i], gath_rs.at[a, o], peer(to)
        )

    def go(a, *which):
        for i in which:
            to, copy = gather_copy(a, i)

            @pl.when(to != o)
            def _(copy=copy):
                copy.start()

    def sibling_copy(a, i, parity):
        block = gath.at[a, 2 * mod8(o + z + REL[i]) + parity]
        return remote(block, block, sib_ss.at[a, i], sib_rs.at[a, i], sibling)

    def forward(a, *which):
        for i in which:
            source = mod8(o + z + REL[i])
            block = gath.at[a, 2 * source + p]

            @pl.when(source != o)
            def _(source=source, block=block, i=i):
                remote(
                    block, block, gath_ss.at[a, i], gath_rs.at[a, source], sibling
                ).wait_recv()

            sibling_copy(a, i, p).start()

    def tokens(a, *which):
        blocks = []
        for i in which:
            source = mod8(o + z + REL[i])
            blocks += [gath[a, 2 * source], gath[a, 2 * source + 1]]
        return jnp.concatenate(blocks, axis=0)

    def slots(t):
        return {0: (0,), 1: (1, 2), 2: (3, 4), 3: (5, 6), 4: (7,)}[t]

    def compute(a, t):
        for i in slots(t):
            sibling_copy(a, i, 1 - p).wait_recv()
        left = tokens(a, *slots(t))
        if a == 0:
            terms = dot(left, wu[...], 1, 0)
        else:
            terms = dot(left, wd[...], 1, 1)
        part[(t + a) % 2, pl.ds(0, 256 * len(slots(t))), :] = terms

    def ring_copy(a, t, d, j, h):
        at = (a, d, t, 2 * j + h)
        return remote(rs_out.at[at], rs_in.at[at], rs_ss.at[at], rs_rs.at[at], along[d])

    def chunk(a, t, d, j, h):
        rows = pl.ds((256 * d if t else 0) + 128 * j + HALF * h, HALF)
        total = part[(t + a) % 2, rows, :]
        if t > 1 or (t == 1 and h == d):
            ring_copy(a, t - 1, d, j, h).wait_recv()
            total += rs_in[a, d, t - 1, 2 * j + h].astype(F32)
        rs_out[a, d, t, 2 * j + h] = total.astype(BF)
        ring_copy(a, t, d, j, h).start()

    def first(a):
        for j in range(2):
            for d in range(2):
                chunk(a, 0, d, j, d)

    def group(a, t, j):
        for h in range(2):
            chunk(a, t, 0, j, h)
            chunk(a, t, 1, j, 1 - h)

    def last(a):
        for j, h in PARTS:
            rows = pl.ds(128 * j + HALF * h, HALF)
            total = part[a, rows, :]
            for d in range(2):
                ring_copy(a, 3, d, j, h).wait_recv()
                total += rs_in[a, d, 3, 2 * j + h].astype(F32)
            fin[a, rows, :] = total
            y_out[a, rows, :] = total.astype(BF)
        y_copy(a).start()

    def y_copy(a):
        return remote(
            y_out.at[a, pl.ds((1 - yh) * 128, 128)], y_in.at[a], y_ss.at[a], y_rs.at[a], partner
        )

    def reduced(a):
        y_copy(a).wait_recv()
        return fin[a, pl.ds(yh * 128, 128), :] + y_in[a].astype(F32)

    def agy_copy(a, j):
        block = ag.at[a, z, j]
        return remote(block, block, agy_ss.at[a], agy_rs.at[a], partner)

    def zed(d, t):
        return mod8(z - t) if d == 0 else mod8(z + t)

    def ag_copy(a, t, d, j, h, source):
        piece = ag.at[a, zed(d, source), j, pl.ds(h * HALF, HALF)]
        at = (a, d, t - 1, 2 * j + h)
        return remote(piece, piece, ag_ss.at[at], ag_rs.at[at], along[d])

    def ag_own(a, value):
        ag[a, z, yh] = value.astype(BF)
        agy_copy(a, yh).start()

    def ag_first(a):
        for j in (yh, 1 - yh):
            for h in range(2):
                for d in range(2):
                    ag_copy(a, 1, d, j, h, 0).start()
            if j is yh:
                agy_copy(a, 1 - yh).wait_recv()

    def ag_group(a, t, j):
        for h in range(2):
            for d in (h, 1 - h):
                if t < 4 or h == d:
                    ag_copy(a, t, d, j, h, t).wait_recv()
                if t < 3 or (t == 3 and h == d):
                    ag_copy(a, t + 1, d, j, h, t).start()

    def near(t):
        return {0: (7,), 1: (5, 6), 2: (3, 4), 3: (1, 2), 4: (0,)}[t]

    def gathered(a, t):
        blocks = []
        for i in near(t):
            source = mod8(z + REL[i])
            blocks += [ag[a, source, 0], ag[a, source, 1]]
        return jnp.concatenate(blocks, axis=0)

    def accumulate(acc, left, right, start):
        for m in range(3):
            rows = pl.ds(m * 256, 256)
            term = dot(left[:, m * 256 : (m + 1) * 256], right, 0, 0)
            if start:
                acc[rows, :] = term
            else:
                acc[rows, :] += term

    def add_down(t):
        accumulate(acc_down, gathered(0, t), tokens(1, *near(t)), t == 0)

    def add_up(t):
        accumulate(acc_up, tokens(0, *near(t)), gathered(1, t), t == 0)

    def gi_sib_copy(i):
        return remote(
            gi_sib_out.at[i], gi_sib_in.at[i], gs_ss.at[i], gs_rs.at[i], sibling
        )

    def gi_copy(i):
        return remote(
            gi_out.at[i], gi_in.at[o], gi_ss.at[i], gi_rs.at[o], peer(mod8(o + z + REL[i]))
        )

    def gi_start(t):
        part[t % 2, pl.ds(0, 256 * len(near(t))), :] = dot(gathered(1, t), wu[...], 1, 1)
        for n, i in enumerate(near(t)):
            rows = pl.ds(n * 256 + (1 - p) * 128, 128)
            gi_sib_out[i] = part[t % 2, rows, :].astype(BF)
            gi_sib_copy(i).start()

    def gi_finish(t):
        for n, i in enumerate(near(t)):
            gi_sib_copy(i).wait_recv()
            rows = pl.ds(n * 256 + p * 128, 128)
            total = (part[t % 2, rows, :] + gi_sib_in[i].astype(F32)).astype(BF)
            dest = mod8(o + z + REL[i])

            @pl.when(dest == o)
            def _(total=total):
                gi_in[o] = total

            @pl.when(dest != o)
            def _(total=total, i=i):
                gi_out[i] = total
                gi_copy(i).start()

    go(0, 0)
    forward(0, 0)
    go(0, 1, 2)
    w_copies[0].wait()
    compute(0, 0)
    first(0)
    forward(0, 1, 2)
    go(0, 3, 4)
    compute(0, 1)
    group(0, 1, 0)
    go(0, 5, 6)
    forward(0, 3, 4)
    group(0, 1, 1)
    compute(0, 2)
    group(0, 2, 0)
    go(0, 7)
    go(1, 0)
    forward(0, 5, 6)
    group(0, 2, 1)
    compute(0, 3)
    group(0, 3, 0)
    go(1, 1, 2)
    forward(0, 7)
    forward(1, 0)
    group(0, 3, 1)
    compute(0, 4)
    go(1, 3, 4)

    w_copies[1].wait()
    compute(1, 0)
    first(1)
    forward(1, 1, 2)
    last(0)
    compute(1, 1)
    group(1, 1, 0)
    go(1, 5, 6)
    forward(1, 3, 4)
    group(1, 1, 1)
    compute(1, 2)
    group(1, 2, 0)
    go(1, 7)
    forward(1, 5, 6)
    group(1, 2, 1)
    compute(1, 3)
    value, slope = gelu_parts(reduced(0))
    slope_ref[...] = slope
    ag_own(0, value)
    group(1, 3, 0)
    forward(1, 7)
    group(1, 3, 1)
    compute(1, 4)
    ag_first(0)
    last(1)

    add_down(0)
    ag_group(0, 1, 0)
    ag_group(0, 1, 1)
    ag_own(1, reduced(1) * slope_ref[...])
    add_down(1)
    ag_group(0, 2, 0)
    ag_group(0, 2, 1)
    add_down(2)
    ag_group(0, 3, 0)
    ag_group(0, 3, 1)
    ag_first(1)
    add_down(3)
    ag_group(0, 4, 0)
    ag_group(0, 4, 1)

    gi_start(0)
    add_up(0)
    gi_finish(0)
    ag_group(1, 1, 0)
    add_down(4)
    ag_group(1, 1, 1)
    gi_start(1)
    add_up(1)
    ag_group(1, 2, 0)
    gi_finish(1)
    ag_group(1, 2, 1)
    gi_start(2)
    add_up(2)
    ag_group(1, 3, 0)
    gi_finish(2)
    ag_group(1, 3, 1)
    gi_start(3)
    add_up(3)
    gi_finish(3)
    ag_group(1, 4, 0)
    ag_group(1, 4, 1)
    gi_start(4)
    add_up(4)
    gi_finish(4)
    factor = 1.0 / math.sqrt(2048)
    gd_ref[...] = (acc_down[...] * factor).astype(BF)
    gu_ref[...] = (acc_up[...] * factor).astype(BF)

    total = gi_in[o].astype(F32)
    for k in range(1, 8):
        source = mod8(o + k)
        remote(
            gi_out.at[0], gi_in.at[source], gi_ss.at[0], gi_rs.at[source], sibling
        ).wait_recv()
        total += gi_in[source].astype(F32)
    gi_ref[...] = total.astype(BF)

    for a in range(2):
        y_copy(a).wait_send()
        agy_copy(a, yh).wait_send()
        for i in range(8):
            to, copy = gather_copy(a, i)

            @pl.when(to != o)
            def _(copy=copy):
                copy.wait_send()

            sibling_copy(a, i, p).wait_send()
        for d in range(2):
            for j, h in PARTS:
                for t in range(4):
                    if t > 0 or h == d:
                        ring_copy(a, t, d, j, h).wait_send()
                    if t < 3 or h == d:
                        ag_copy(a, t + 1, d, j, h, t).wait_send()
    for i in range(8):
        gi_sib_copy(i).wait_send()

        @pl.when(mod8(o + z + REL[i]) != o)
        def _(i=i):
            gi_copy(i).wait_send()


def on_device(inputs, w_up, w_down, upstream):
    tokens, width = inputs.shape
    hidden = w_up.shape[1]
    dma = pltpu.SemaphoreType.DMA
    vmem = pl.BlockSpec(memory_space=pltpu.VMEM)
    anywhere = pl.BlockSpec(memory_space=pl.ANY)
    return pl.pallas_call(
        kernel,
        out_shape=(
            jax.ShapeDtypeStruct((tokens, width), BF),
            jax.ShapeDtypeStruct((width, hidden), BF),
            jax.ShapeDtypeStruct((hidden, width), BF),
        ),
        in_specs=[vmem, anywhere, anywhere, vmem],
        out_specs=(vmem, vmem, vmem),
        scratch_shapes=[
            pltpu.VMEM((2, 16, 128, 768), BF),
            pltpu.VMEM((2, 512, 768), F32),
            pltpu.VMEM((768, 768), BF),
            pltpu.VMEM((768, 768), BF),
            pltpu.VMEM((2, 2, 4, 4, HALF, 768), BF),
            pltpu.VMEM((2, 2, 4, 4, HALF, 768), BF),
            pltpu.VMEM((2, 256, 768), F32),
            pltpu.VMEM((2, 256, 768), BF),
            pltpu.VMEM((2, 128, 768), BF),
            pltpu.VMEM((128, 768), F32),
            pltpu.VMEM((2, 8, 2, 128, 768), BF),
            pltpu.VMEM((768, 768), F32),
            pltpu.VMEM((768, 768), F32),
            pltpu.VMEM((8, 128, 768), BF),
            pltpu.VMEM((8, 128, 768), BF),
            pltpu.VMEM((8, 128, 768), BF),
            pltpu.VMEM((8, 128, 768), BF),
            dma((2,)), dma((2, 8)), dma((2, 8)), dma((2, 8)), dma((2, 8)),
            dma((2, 2, 4, 4)), dma((2, 2, 4, 4)),
            dma((2,)), dma((2,)), dma((2,)), dma((2,)),
            dma((2, 2, 4, 4)), dma((2, 2, 4, 4)),
            dma((8,)), dma((8,)), dma((8,)), dma((8,)),
        ],
        compiler_params=pltpu.CompilerParams(
            collective_id=0, has_side_effects=True, vmem_limit_bytes=58 << 20
        ),
        cost_estimate=pl.CostEstimate(
            flops=5 * 2 * 2048 * 768 * 768, bytes_accessed=6 << 20, transcendentals=128 * 768
        ),
        name="block_backward",
    )(inputs, w_up, w_down, upstream)


def solution(mesh):
    in_specs = (P("row", "col"), P("col", "row"), P("row", "col"), P("row", "col"))
    out_specs = (P("row", "col"), P("col", "row"), P("row", "col"))
    return jax.shard_map(
        on_device, mesh=mesh, in_specs=in_specs, out_specs=out_specs, check_vma=False
    )
```

time: 780 us -> 173 us (0.22)
  the two profiles are of different devices: /device:TPU:6 before, /device:TPU:25 now
where the time goes in v2:
time: 173 us
  Pallas kernels  167 us (97%)
  local copies, waits for them, and re-layouts  5.09 us (3%)
    pallas_call x1, Pallas kernels, on_device(): pl.pallas_call(kernel, out_shape=(jax.ShapeDtypeStruct((tokens, width), B...  167 us
    unnamed x5, local copies, waits for them, and re-layouts  5.09 us

profile of v2, /device:TPU:25, one launch (start us, length us, event | category | flops | bytes accessed | tf_op | source)
XLA Modules:
  0.0 172.9 jit_solution(17873410084259221700)
XLA Ops:
  0.6 167.1 %block_backward.1 = (bf16[128,768]{1,0:T(8,128)(2,1)}, bf16[768,768]{1,0:T(8,128)(2,1)}, bf16[768,768]{1,0:T(8,128)(2,1)}) custom-call(bf16[128,768]{1,0:T(8,128)(2,1)} %x_ref.1, bf16[768,768]{1,0:T(8,128)(2,1)} %wu_ref.1, bf16[768,768]{1,0:T(8,128)(2,1)} %wd_ref.1, bf16[128,768]{1,0:T(8,128)(2,1)} %g_ref.1), custom_call_target="tpu_custom_call" | custom-call | flops 12079595520 | bytes 6291456 | tf_op jit(solution)/shard_map/block_backward/pallas_call | solution.py:405
  167.8 1.6 copy.10
  169.4 0.0 copy-start
  169.4 2.5 %copy.11 = bf16[768,768]{1,0:T(8,128)(2,1)} copy(bf16[768,768]{1,0:T(8,128)(2,1)} %get-tuple-element.7) | data formatting | bytes 2359296
  171.8 0.0 copy-done
  171.9 1.0 copy.12
Async XLA Ops:
  169.4 2.5 %copy-start = (bf16[768,768]{1,0:T(8,128)(2,1)S(1)}, bf16[768,768]{1,0:T(8,128)(2,1)}, u32[]{:S(2)}) copy-start(bf16[768,768]{1,0:T(8,128)(2,1)} %get-tuple-element.8) | copy-start | bytes 3538948

commit v3 on v2

--- a/solution.py
+++ b/solution.py
@@ -11,7 +11,6 @@
 MESH = pl.DeviceIdType.MESH
 BF = jnp.bfloat16
 F32 = jnp.float32
-RING = 8
 HALF = 64
 REL = (4, 3, -3, 2, -2, 1, -1, 0)
 PARTS = tuple((j, h) for j in range(2) for h in range(2))
@@ -41,10 +40,10 @@
 
 def kernel(
     x_ref, wu_ref, wd_ref, g_ref,
-    gi_ref, gu_ref, gd_ref,
-    gath, part, wu, wd, rs_out, rs_in, fin, y_out, y_in, slope_ref, ag, acc_up, acc_down,
+    gi_hbm, gu_hbm, gd_hbm,
+    gi_ref, gu_ref, gd_ref, gath, part, wu, wd, rs_out, rs_in, fin, y_out, y_in, slope_ref, ag, acc_up, acc_down,
     gi_sib_out, gi_sib_in, gi_out, gi_in,
-    w_sem, gath_ss, gath_rs, sib_ss, sib_rs, rs_ss, rs_rs, y_ss, y_rs,
+    out_sem, w_sem, gath_ss, gath_rs, sib_ss, sib_rs, rs_ss, rs_rs, y_ss, y_rs,
     agy_ss, agy_rs, ag_ss, ag_rs, gs_ss, gs_rs, gi_ss, gi_rs,
 ):
     r, c = lax.axis_index("row"), lax.axis_index("col")
@@ -190,13 +189,14 @@
         ag[a, z, yh] = value.astype(BF)
         agy_copy(a, yh).start()
 
-    def ag_first(a):
-        for j in (yh, 1 - yh):
-            for h in range(2):
-                for d in range(2):
-                    ag_copy(a, 1, d, j, h, 0).start()
-            if j is yh:
-                agy_copy(a, 1 - yh).wait_recv()
+    def ag_first(a, j):
+        @pl.when(yh != j)
+        def _():
+            agy_copy(a, j).wait_recv()
+
+        for h in range(2):
+            for d in range(2):
+                ag_copy(a, 1, d, j, h, 0).start()
 
     def ag_group(a, t, j):
         for h in range(2):
@@ -216,20 +216,39 @@
             blocks += [ag[a, source, 0], ag[a, source, 1]]
         return jnp.concatenate(blocks, axis=0)
 
-    def accumulate(acc, left, right, start):
+    def add_down(j, t):
+        left = jnp.concatenate([ag[0, mod8(z + REL[i]), j] for i in near(t)], axis=0)
+        right = jnp.concatenate(
+            [gath[1, 2 * mod8(o + z + REL[i]) + j] for i in near(t)], axis=0
+        )
         for m in range(3):
             rows = pl.ds(m * 256, 256)
             term = dot(left[:, m * 256 : (m + 1) * 256], right, 0, 0)
-            if start:
-                acc[rows, :] = term
+            if (j, t) == (0, 0):
+                acc_down[rows, :] = term
+            elif (j, t) != (1, 4):
+                acc_down[rows, :] += term
             else:
-                acc[rows, :] += term
-
-    def add_down(t):
-        accumulate(acc_down, gathered(0, t), tokens(1, *near(t)), t == 0)
+                gd_ref[rows, :] = ((acc_down[rows, :] + term) * factor).astype(BF)
+                out_copy(2 + m).start()
 
     def add_up(t):
-        accumulate(acc_up, tokens(0, *near(t)), gathered(1, t), t == 0)
+        left, right = tokens(0, *near(t)), gathered(1, t)
+        for m in range(3):
+            rows = pl.ds(m * 256, 256)
+            term = dot(left[:, m * 256 : (m + 1) * 256], right, 0, 0)
+            if t == 0:
+                acc_up[rows, :] = term
+            else:
+                acc_up[rows, :] += term
+
+    def out_copy(n):
+        if n == 0:
+            return pltpu.make_async_copy(gi_ref, gi_hbm, out_sem.at[0])
+        if n == 1:
+            return pltpu.make_async_copy(gu_ref, gu_hbm, out_sem.at[1])
+        rows = pl.ds((n - 2) * 256, 256)
+        return pltpu.make_async_copy(gd_ref.at[rows], gd_hbm.at[rows], out_sem.at[n])
 
     def gi_sib_copy(i):
         return remote(
@@ -315,29 +334,27 @@
     forward(1, 7)
     group(1, 3, 1)
     compute(1, 4)
-    ag_first(0)
+    ag_first(0, 0)
     last(1)
 
-    add_down(0)
+    factor = 1.0 / math.sqrt(2048)
+    add_down(0, 0)
     ag_group(0, 1, 0)
-    ag_group(0, 1, 1)
     ag_own(1, reduced(1) * slope_ref[...])
-    add_down(1)
+    add_down(0, 1)
     ag_group(0, 2, 0)
-    ag_group(0, 2, 1)
-    add_down(2)
+    add_down(0, 2)
     ag_group(0, 3, 0)
-    ag_group(0, 3, 1)
-    ag_first(1)
-    add_down(3)
+    ag_first(1, 0)
+    ag_first(1, 1)
+    add_down(0, 3)
     ag_group(0, 4, 0)
-    ag_group(0, 4, 1)
 
     gi_start(0)
     add_up(0)
     gi_finish(0)
     ag_group(1, 1, 0)
-    add_down(4)
+    add_down(0, 4)
     ag_group(1, 1, 1)
     gi_start(1)
     add_up(1)
@@ -349,18 +366,25 @@
     ag_group(1, 3, 0)
     gi_finish(2)
     ag_group(1, 3, 1)
+    ag_first(0, 1)
     gi_start(3)
     add_up(3)
     gi_finish(3)
     ag_group(1, 4, 0)
     ag_group(1, 4, 1)
     gi_start(4)
+    ag_group(0, 1, 1)
+    gi_finish(4)
     add_up(4)
-    gi_finish(4)
-    factor = 1.0 / math.sqrt(2048)
-    gd_ref[...] = (acc_down[...] * factor).astype(BF)
+
     gu_ref[...] = (acc_up[...] * factor).astype(BF)
-
+    out_copy(1).start()
+    add_down(1, 0)
+    add_down(1, 1)
+    ag_group(0, 2, 1)
+    add_down(1, 2)
+    ag_group(0, 3, 1)
+    add_down(1, 3)
     total = gi_in[o].astype(F32)
     for k in range(1, 8):
         source = mod8(o + k)
@@ -369,7 +393,12 @@
         ).wait_recv()
         total += gi_in[source].astype(F32)
     gi_ref[...] = total.astype(BF)
-
+    out_copy(0).start()
+    ag_group(0, 4, 1)
+    add_down(1, 4)
+
+    for n in range(5):
+        out_copy(n).wait()
     for a in range(2):
         y_copy(a).wait_send()
         agy_copy(a, yh).wait_send()
@@ -396,7 +425,43 @@
             gi_copy(i).wait_send()
 
 
-def on_device(inputs, w_up, w_down, upstream):
+def copy_kernel(*refs):
+    sources, targets, stages, sem = refs[:3], refs[3:6], refs[6:9], refs[9]
+    pieces = [(0, 0, 128)] + [(n, m * 256, 256) for n in (1, 2) for m in range(3)]
+
+    def copies(k):
+        n, start, extent = pieces[k]
+        rows = pl.ds(start, extent)
+        return (
+            pltpu.make_async_copy(sources[n].at[rows], stages[n].at[rows], sem.at[0, k]),
+            pltpu.make_async_copy(stages[n].at[rows], targets[n].at[rows], sem.at[1, k]),
+        )
+
+    for k in range(len(pieces)):
+        copies(k)[0].start()
+    for k in range(len(pieces)):
+        copies(k)[0].wait()
+        copies(k)[1].start()
+    for k in range(len(pieces)):
+        copies(k)[1].wait()
+
+
+def on_device(*args):
+    results = block(*args)
+    anywhere = pl.BlockSpec(memory_space=pl.ANY)
+    return pl.pallas_call(
+        copy_kernel,
+        out_shape=tuple(jax.ShapeDtypeStruct(t.shape, t.dtype) for t in results),
+        in_specs=[anywhere] * 3,
+        out_specs=(anywhere,) * 3,
+        scratch_shapes=[pltpu.VMEM(t.shape, t.dtype) for t in results]
+        + [pltpu.SemaphoreType.DMA((2, 7))],
+        compiler_params=pltpu.CompilerParams(vmem_limit_bytes=58 << 20),
+        name="hand_over",
+    )(*results)
+
+
+def block(inputs, w_up, w_down, upstream):
     tokens, width = inputs.shape
     hidden = w_up.shape[1]
     dma = pltpu.SemaphoreType.DMA
@@ -410,8 +475,11 @@
             jax.ShapeDtypeStruct((hidden, width), BF),
         ),
         in_specs=[vmem, anywhere, anywhere, vmem],
-        out_specs=(vmem, vmem, vmem),
+        out_specs=(anywhere, anywhere, anywhere),
         scratch_shapes=[
+            pltpu.VMEM((tokens, width), BF),
+            pltpu.VMEM((width, hidden), BF),
+            pltpu.VMEM((hidden, width), BF),
             pltpu.VMEM((2, 16, 128, 768), BF),
             pltpu.VMEM((2, 512, 768), F32),
             pltpu.VMEM((768, 768), BF),
@@ -429,7 +497,7 @@
             pltpu.VMEM((8, 128, 768), BF),
             pltpu.VMEM((8, 128, 768), BF),
             pltpu.VMEM((8, 128, 768), BF),
-            dma((2,)), dma((2, 8)), dma((2, 8)), dma((2, 8)), dma((2, 8)),
+            dma((5,)), dma((2,)), dma((2, 8)), dma((2, 8)), dma((2, 8)), dma((2, 8)),
             dma((2, 2, 4, 4)), dma((2, 2, 4, 4)),
             dma((2,)), dma((2,)), dma((2,)), dma((2,)),
             dma((2, 2, 4, 4)), dma((2, 2, 4, 4)),

time: 173 us -> 162 us (0.936)
  the two profiles are of different devices: /device:TPU:25 before, /device:TPU:6 now
where the time goes in v3:
time: 162 us
  Pallas kernels  161 us (99%)
    pallas_call x1, Pallas kernels, block(): pl.pallas_call(kernel, out_shape=(jax.ShapeDtypeStruct((tokens, width), B...  158 us

profile of v3, /device:TPU:6, one launch (start us, length us, event | category | flops | bytes accessed | tf_op | source)
XLA Modules:
  0.0 161.6 jit_solution(9526794503693984378)
XLA Ops:
  0.6 158.2 %block_backward.1 = (bf16[128,768]{1,0:T(8,128)(2,1)}, bf16[768,768]{1,0:T(8,128)(2,1)}, bf16[768,768]{1,0:T(8,128)(2,1)}) custom-call(bf16[128,768]{1,0:T(8,128)(2,1)} %x_ref.1, bf16[768,768]{1,0:T(8,128)(2,1)} %wu_ref.1, bf16[768,768]{1,0:T(8,128)(2,1)} %wd_ref.1, bf16[128,768]{1,0:T(8,128)(2,1)} %g_ref.1), custom_call_target="tpu_custom_call" | custom-call | flops 12079595520 | bytes 6291456 | tf_op jit(solution)/shard_map/block_backward/pallas_call | solution.py:470
  158.8 2.6 %hand_over.1 = (bf16[128,768]{1,0:T(8,128)(2,1)}, bf16[768,768]{1,0:T(8,128)(2,1)}, bf16[768,768]{1,0:T(8,128)(2,1)}) custom-call(bf16[128,768]{1,0:T(8,128)(2,1)} %get-tuple-element.6.refs_0_, bf16[768,768]{1,0:T(8,128)(2,1)} %get-tuple-element.7.refs_1_, bf16[768,768]{1,0:T(8,128)(2,1)} %get-tuple-element.8.refs_2_), custom_call_target="tpu_custom_call" | custom-call | tf_op jit(solution)/shard_map/hand_over/pallas_call | solution.py:452

commit v4 on v3

--- a/solution.py
+++ b/solution.py
@@ -154,28 +154,31 @@
             chunk(a, t, 1, j, 1 - h)
 
     def last(a):
-        for j, h in PARTS:
-            rows = pl.ds(128 * j + HALF * h, HALF)
-            total = part[a, rows, :]
-            for d in range(2):
-                ring_copy(a, 3, d, j, h).wait_recv()
-                total += rs_in[a, d, 3, 2 * j + h].astype(F32)
-            fin[a, rows, :] = total
-            y_out[a, rows, :] = total.astype(BF)
-        y_copy(a).start()
-
-    def y_copy(a):
+        for h in range(2):
+            for j in range(2):
+                rows = pl.ds(128 * j + HALF * h, HALF)
+                total = part[a, rows, :]
+                for d in range(2):
+                    ring_copy(a, 3, d, j, h).wait_recv()
+                    total += rs_in[a, d, 3, 2 * j + h].astype(F32)
+                fin[a, rows, :] = total
+                y_out[a, rows, :] = total.astype(BF)
+            y_copy(a, h).start()
+
+    def y_copy(a, h):
         return remote(
-            y_out.at[a, pl.ds((1 - yh) * 128, 128)], y_in.at[a], y_ss.at[a], y_rs.at[a], partner
-        )
-
-    def reduced(a):
-        y_copy(a).wait_recv()
-        return fin[a, pl.ds(yh * 128, 128), :] + y_in[a].astype(F32)
-
-    def agy_copy(a, j):
-        block = ag.at[a, z, j]
-        return remote(block, block, agy_ss.at[a], agy_rs.at[a], partner)
+            y_out.at[a, pl.ds((1 - yh) * 128 + HALF * h, HALF)],
+            y_in.at[a, pl.ds(HALF * h, HALF)], y_ss.at[a, h], y_rs.at[a, h], partner,
+        )
+
+    def reduced(a, h):
+        y_copy(a, h).wait_recv()
+        own = fin[a, pl.ds(yh * 128 + HALF * h, HALF), :]
+        return own + y_in[a, pl.ds(HALF * h, HALF), :].astype(F32)
+
+    def agy_copy(a, j, h):
+        piece = ag.at[a, z, j, pl.ds(HALF * h, HALF)]
+        return remote(piece, piece, agy_ss.at[a, h], agy_rs.at[a, h], partner)
 
     def zed(d, t):
         return mod8(z - t) if d == 0 else mod8(z + t)
@@ -185,18 +188,25 @@
         at = (a, d, t - 1, 2 * j + h)
         return remote(piece, piece, ag_ss.at[at], ag_rs.at[at], along[d])
 
-    def ag_own(a, value):
-        ag[a, z, yh] = value.astype(BF)
-        agy_copy(a, yh).start()
+    def ag_own(a, h, value):
+        ag[a, z, yh, pl.ds(HALF * h, HALF), :] = value.astype(BF)
+        agy_copy(a, yh, h).start()
 
     def ag_first(a, j):
-        @pl.when(yh != j)
-        def _():
-            agy_copy(a, j).wait_recv()
-
         for h in range(2):
-            for d in range(2):
-                ag_copy(a, 1, d, j, h, 0).start()
+            if a == 1:
+                agy_copy(1, j, h).wait_recv()
+            else:
+
+                @pl.when(yh != j)
+                def _(h=h):
+                    agy_copy(0, j, h).wait_recv()
+
+            ag_begin(a, j, h)
+
+    def ag_begin(a, j, h):
+        for d in range(2):
+            ag_copy(a, 1, d, j, h, 0).start()
 
     def ag_group(a, t, j):
         for h in range(2):
@@ -283,53 +293,53 @@
                 gi_out[i] = total
                 gi_copy(i).start()
 
-    go(0, 0)
+    go(0, 0, 1, 2)
     forward(0, 0)
-    go(0, 1, 2)
     w_copies[0].wait()
     compute(0, 0)
     first(0)
+    go(0, 3, 4)
     forward(0, 1, 2)
-    go(0, 3, 4)
+    go(0, 5, 6)
     compute(0, 1)
     group(0, 1, 0)
-    go(0, 5, 6)
     forward(0, 3, 4)
+    go(0, 7)
     group(0, 1, 1)
     compute(0, 2)
+    go(1, 0)
     group(0, 2, 0)
-    go(0, 7)
-    go(1, 0)
     forward(0, 5, 6)
+    go(1, 1, 2)
     group(0, 2, 1)
     compute(0, 3)
+    forward(0, 7)
     group(0, 3, 0)
-    go(1, 1, 2)
-    forward(0, 7)
     forward(1, 0)
+    go(1, 3, 4)
     group(0, 3, 1)
     compute(0, 4)
-    go(1, 3, 4)
 
     w_copies[1].wait()
     compute(1, 0)
     first(1)
     forward(1, 1, 2)
+    go(1, 5, 6)
     last(0)
     compute(1, 1)
     group(1, 1, 0)
-    go(1, 5, 6)
     forward(1, 3, 4)
+    go(1, 7)
     group(1, 1, 1)
     compute(1, 2)
     group(1, 2, 0)
-    go(1, 7)
     forward(1, 5, 6)
     group(1, 2, 1)
     compute(1, 3)
-    value, slope = gelu_parts(reduced(0))
-    slope_ref[...] = slope
-    ag_own(0, value)
+    for h in range(2):
+        value, slope = gelu_parts(reduced(0, h))
+        slope_ref[pl.ds(HALF * h, HALF), :] = slope
+        ag_own(0, h, value)
     group(1, 3, 0)
     forward(1, 7)
     group(1, 3, 1)
@@ -340,13 +350,15 @@
     factor = 1.0 / math.sqrt(2048)
     add_down(0, 0)
     ag_group(0, 1, 0)
-    ag_own(1, reduced(1) * slope_ref[...])
+    for h in range(2):
+        ag_own(1, h, reduced(1, h) * slope_ref[pl.ds(HALF * h, HALF), :])
     add_down(0, 1)
     ag_group(0, 2, 0)
+    for h in range(2):
+        ag_begin(1, yh, h)
     add_down(0, 2)
     ag_group(0, 3, 0)
-    ag_first(1, 0)
-    ag_first(1, 1)
+    ag_first(1, 1 - yh)
     add_down(0, 3)
     ag_group(0, 4, 0)
 
@@ -358,13 +370,13 @@
     ag_group(1, 1, 1)
     gi_start(1)
     add_up(1)
+    gi_finish(1)
     ag_group(1, 2, 0)
-    gi_finish(1)
     ag_group(1, 2, 1)
     gi_start(2)
     add_up(2)
+    gi_finish(2)
     ag_group(1, 3, 0)
-    gi_finish(2)
     ag_group(1, 3, 1)
     ag_first(0, 1)
     gi_start(3)
@@ -385,6 +397,8 @@
     add_down(1, 2)
     ag_group(0, 3, 1)
     add_down(1, 3)
+    ag_group(0, 4, 1)
+    add_down(1, 4)
     total = gi_in[o].astype(F32)
     for k in range(1, 8):
         source = mod8(o + k)
@@ -394,14 +408,13 @@
         total += gi_in[source].astype(F32)
     gi_ref[...] = total.astype(BF)
     out_copy(0).start()
-    ag_group(0, 4, 1)
-    add_down(1, 4)
 
     for n in range(5):
         out_copy(n).wait()
     for a in range(2):
-        y_copy(a).wait_send()
-        agy_copy(a, yh).wait_send()
+        for h in range(2):
+            y_copy(a, h).wait_send()
+            agy_copy(a, yh, h).wait_send()
         for i in range(8):
             to, copy = gather_copy(a, i)
 
@@ -499,7 +512,7 @@
             pltpu.VMEM((8, 128, 768), BF),
             dma((5,)), dma((2,)), dma((2, 8)), dma((2, 8)), dma((2, 8)), dma((2, 8)),
             dma((2, 2, 4, 4)), dma((2, 2, 4, 4)),
-            dma((2,)), dma((2,)), dma((2,)), dma((2,)),
+            dma((2, 2)), dma((2, 2)), dma((2, 2)), dma((2, 2)),
             dma((2, 2, 4, 4)), dma((2, 2, 4, 4)),
             dma((8,)), dma((8,)), dma((8,)), dma((8,)),
         ],

time: 162 us -> 156 us (0.963)
  Pallas kernels: 161 us -> 155 us
    pallas_call x1, Pallas kernels: 158 us -> 152 us  [block(): pl.pallas_call(kernel, out_shape=(jax.ShapeDtypeStruct((tokens, width), B...]
where the time goes in v4:
time: 156 us
  Pallas kernels  155 us (99%)
    pallas_call x1, Pallas kernels, block(): pl.pallas_call(kernel, out_shape=(jax.ShapeDtypeStruct((tokens, width), B...  152 us

profile of v4, /device:TPU:6, one launch (start us, length us, event | category | flops | bytes accessed | tf_op | source)
XLA Modules:
  0.0 155.8 jit_solution(6098883995261747215)
XLA Ops:
  0.6 152.4 %block_backward.1 = (bf16[128,768]{1,0:T(8,128)(2,1)}, bf16[768,768]{1,0:T(8,128)(2,1)}, bf16[768,768]{1,0:T(8,128)(2,1)}) custom-call(bf16[128,768]{1,0:T(8,128)(2,1)} %x_ref.1, bf16[768,768]{1,0:T(8,128)(2,1)} %wu_ref.1, bf16[768,768]{1,0:T(8,128)(2,1)} %wd_ref.1, bf16[128,768]{1,0:T(8,128)(2,1)} %g_ref.1), custom_call_target="tpu_custom_call" | custom-call | flops 12079595520 | bytes 6291456 | tf_op jit(solution)/shard_map/block_backward/pallas_call | solution.py:483
  153.0 2.6 %hand_over.1 = (bf16[128,768]{1,0:T(8,128)(2,1)}, bf16[768,768]{1,0:T(8,128)(2,1)}, bf16[768,768]{1,0:T(8,128)(2,1)}) custom-call(bf16[128,768]{1,0:T(8,128)(2,1)} %get-tuple-element.6.refs_0_, bf16[768,768]{1,0:T(8,128)(2,1)} %get-tuple-element.7.refs_1_, bf16[768,768]{1,0:T(8,128)(2,1)} %get-tuple-element.8.refs_2_), custom_call_target="tpu_custom_call" | custom-call | tf_op jit(solution)/shard_map/hand_over/pallas_call | solution.py:465
